TPU v7x, 32 devices: a whole 2x2x4 slice. The times are simulated.
32 devices in a mesh: grp: 4 (over y, x), dp: 8 (over z, core).
Axes of the slice: x: 2, y: 2, z: 4, core: 2. Of those that a mesh axis runs over, the one named last changes fastest.
Arguments:
- features: bfloat16 [32, 1024, 512], P(('grp', 'dp')), may hold values from -6 to 6
- segment_lengths: int32 [32, 4], P(('grp', 'dp')), may hold values from 1 to 512, 1024 in all within a row
- subnet_config: int32 [4, 3], P('grp'), may hold values from 8 to 3072, as said below
- cotangent: bfloat16 [32, 1024, 768], P(('grp', 'dp')), may hold values from -6 to 6
- projection_weight: float32 [512, 768], P(('grp', 'dp')), may hold values from -0.25 to 0.25
- projection_moment: float32 [512, 768], P(('grp', 'dp')), may hold values from -80 to 80
- projection_square: float32 [512, 768], P(('grp', 'dp')), may hold values from 16.384 to 65.536
- attention_weight: float32 [3, 768, 768], P(None, ('grp', 'dp')), may hold values from -0.21875 to 0.21875
- attention_moment: float32 [3, 768, 768], P(None, ('grp', 'dp')), may hold values from -28 to 28
- attention_square: float32 [3, 768, 768], P(None, ('grp', 'dp')), may hold values from 1.6384 to 6.5536
- output_weight: float32 [768, 768], P(('grp', 'dp')), may hold values from -1.75 to 1.75
- output_moment: float32 [768, 768], P(('grp', 'dp')), may hold values from -12 to 12
- output_square: float32 [768, 768], P(('grp', 'dp')), may hold values from 0.32768 to 1.31072
- feedforward_weight: float32 [2, 768, 3072], P(None, ('grp', 'dp')), may hold values from -0.21875 to 0.21875
- feedforward_moment: float32 [2, 768, 3072], P(None, ('grp', 'dp')), may hold values from -48 to 48
- feedforward_square: float32 [2, 768, 3072], P(None, ('grp', 'dp')), may hold values from 4.9152 to 19.6608
- small_params: float32 [11008], P(('grp', 'dp')), may hold values from -0.4 to 1.3, as said below
- small_moment: float32 [11008], P(('grp', 'dp')), may hold values from -80 to 80
- small_square: float32 [11008], P(('grp', 'dp')), may hold values from 16.384 to 65.536
Outputs:
- activations: bfloat16 [32, 1024, 768], P(('grp', 'dp'))
- input_gradient: float32 [32, 1024, 512], P(('grp', 'dp'))
- projection_gradient: float32 [512, 768], P(('grp', 'dp'))
- projection_moment_new: float32 [512, 768], P(('grp', 'dp'))
- projection_square_new: float32 [512, 768], P(('grp', 'dp'))
- projection_updated: float32 [512, 768], P(('grp', 'dp'))
- attention_gradient: float32 [3, 768, 768], P(None, ('grp', 'dp'))
- attention_moment_new: float32 [3, 768, 768], P(None, ('grp', 'dp'))
- attention_square_new: float32 [3, 768, 768], P(None, ('grp', 'dp'))
- attention_updated: float32 [3, 768, 768], P(None, ('grp', 'dp'))
- output_gradient: float32 [768, 768], P(('grp', 'dp'))
- output_moment_new: float32 [768, 768], P(('grp', 'dp'))
- output_square_new: float32 [768, 768], P(('grp', 'dp'))
- output_updated: float32 [768, 768], P(('grp', 'dp'))
- feedforward_gradient: float32 [2, 768, 3072], P(None, ('grp', 'dp'))
- feedforward_moment_new: float32 [2, 768, 3072], P(None, ('grp', 'dp'))
- feedforward_square_new: float32 [2, 768, 3072], P(None, ('grp', 'dp'))
- feedforward_updated: float32 [2, 768, 3072], P(None, ('grp', 'dp'))
- small_gradient: float32 [11008], P(('grp', 'dp'))
- small_moment_new: float32 [11008], P(('grp', 'dp'))
- small_square_new: float32 [11008], P(('grp', 'dp'))
- small_updated: float32 [11008], P(('grp', 'dp'))
Inputs may be any that keep to these rules, and one draw needn't show every extreme that they name: `subnet_config`: each row is (E, H, F) with E one of 512, 640, 768; H one of 8, 10, 12; F = E * k // 2 with k one of 6, 7, 8. Some group has (768, 12, 3072) and some other group (512, 8, 1536). `small_params`: the three gains g0, g1, g2 lie in 0.7 to 1.3, all biases in -0.4 to 0.4.
All inputs are finite; a program needn't handle non-finite values.
Results may differ from a plain program's by a relative error of at most 0.017.
The roundings to bfloat16 on the way count: a program that leaves them out, or rounds other values in their place, can miss the bound.
Values may be sent and summed in bfloat16 or wider, within the bound.
A program may use at most 256 MiB of HBM per device.

v0:
```python
import math

import jax
import jax.numpy as jnp
from jax import lax
from jax.sharding import PartitionSpec as P

D = 768
FF = 3072
FEAT = 512
HDIM = 64
STEP = 10


NORM_EPS = 1e-05
RATE = 0.08
SMALL_RATE = 0.3
BETA_ONE = 0.9
BETA_TWO = 0.999
ADAM_EPS = 1e-08
DECAY = 0.01


def vector_pieces(vector):
    widths = [FEAT, FEAT, D, D, D, D, D, D, FF, D, D, D]
    pieces = []
    offset = 0
    for width in widths:
        pieces.append(vector[offset : offset + width])
        offset = offset + width
    return pieces


def plain_norm(value, gain, shift):
    centre = jnp.mean(value, -1, keepdims=True)
    centred = value - centre
    spread = jnp.mean(centred * centred, -1, keepdims=True)
    return centred * lax.rsqrt(spread + NORM_EPS) * gain + shift


def masked_norm(value, gain, shift, keep, count):
    centre = jnp.sum(value * keep, -1, keepdims=True) / count
    centred = (value - centre) * keep
    spread = jnp.sum(centred * centred, -1, keepdims=True) / count
    return (centred * lax.rsqrt(spread + NORM_EPS) * gain + shift) * keep


def exact_gelu(value):
    return jax.nn.gelu(value, approximate=False)


def attend_row(inputs):
    query, key, value, segment = inputs
    length = query.shape[0]
    block = min(512, length)
    scale = 1.0 / math.sqrt(query.shape[2])
    mixed_parts = []
    totals = []
    for begin in range(0, length, block):
        block_query = query[begin : begin + block]
        same = segment[begin : begin + block, None] == segment[None, :]
        raw = jnp.einsum("qhd,khd->hqk", block_query, key, preferred_element_type=jnp.float32)
        scores = jnp.where(same[None], raw * scale, -1e30)
        peak = jnp.max(scores, -1, keepdims=True)
        powers = jnp.exp(scores - peak)
        summed = jnp.sum(powers, -1, keepdims=True)
        weights = (powers / summed).astype(jnp.bfloat16)
        mixed_parts.append(
            jnp.einsum("hqk,khd->qhd", weights, value, preferred_element_type=jnp.float32)
        )
        totals.append(peak + jnp.log(summed))
    return (jnp.concatenate(mixed_parts, 0), jnp.concatenate(totals, 1))


def attend_back(inputs):
    query, key, value, segment, grad_mixed, totals = inputs
    length = query.shape[0]
    block = min(512, length)
    scale = 1.0 / math.sqrt(query.shape[2])
    key_grad = jnp.zeros(key.shape, jnp.float32)
    value_grad = jnp.zeros(value.shape, jnp.float32)
    query_parts = []
    for begin in range(0, length, block):
        block_query = query[begin : begin + block]
        block_grad = grad_mixed[begin : begin + block]
        same = segment[begin : begin + block, None] == segment[None, :]
        raw = jnp.einsum("qhd,khd->hqk", block_query, key, preferred_element_type=jnp.float32)
        scores = jnp.where(same[None], raw * scale, -1e30)
        weights = jnp.exp(scores - totals[:, begin : begin + block])
        weights_low = weights.astype(jnp.bfloat16)
        weight_grad = jnp.einsum(
            "qhd,khd->hqk", block_grad, value, preferred_element_type=jnp.float32
        )
        inner_sum = jnp.sum(weights * weight_grad, -1, keepdims=True)
        score_grad = weights * (weight_grad - inner_sum)
        raw_grad = (jnp.where(same[None], score_grad, 0.0) * scale).astype(jnp.bfloat16)
        query_parts.append(
            jnp.einsum("hqk,khd->qhd", raw_grad, key, preferred_element_type=jnp.float32)
        )
        key_grad = key_grad + jnp.einsum(
            "hqk,qhd->khd", raw_grad, block_query, preferred_element_type=jnp.float32
        )
        value_grad = value_grad + jnp.einsum(
            "hqk,qhd->khd", weights_low, block_grad, preferred_element_type=jnp.float32
        )
    return (jnp.concatenate(query_parts, 0), key_grad, value_grad)


def adam(weight, moment, square, grad, rate):
    moment_new = BETA_ONE * moment + (1.0 - BETA_ONE) * grad
    square_new = BETA_TWO * square + (1.0 - BETA_TWO) * grad * grad
    fix_one = 1.0 - BETA_ONE**STEP
    fix_two = 1.0 - BETA_TWO**STEP
    direction = moment_new / fix_one / (jnp.sqrt(square_new / fix_two) + ADAM_EPS)
    return (moment_new, square_new, weight - rate * (direction + DECAY * weight))


def per_device(
    features,
    segment_lengths,
    subnet_config,
    cotangent,
    projection_weight,
    projection_moment,
    projection_square,
    attention_weight,
    attention_moment,
    attention_square,
    output_weight,
    output_moment,
    output_square,
    feedforward_weight,
    feedforward_moment,
    feedforward_square,
    small_params,
    small_moment,
    small_square,
):
    projection_copy, attention_copy, output_copy, feedforward_copy, small_copy = (
        lax.all_gather(projection_weight.astype(jnp.bfloat16), ("grp", "dp"), axis=0, tiled=True),
        lax.all_gather(attention_weight.astype(jnp.bfloat16), ("grp", "dp"), axis=1, tiled=True),
        lax.all_gather(output_weight.astype(jnp.bfloat16), ("grp", "dp"), axis=0, tiled=True),
        lax.all_gather(feedforward_weight.astype(jnp.bfloat16), ("grp", "dp"), axis=1, tiled=True),
        lax.all_gather(small_params.astype(jnp.bfloat16), ("grp", "dp"), axis=0, tiled=True),
    )
    vector = small_copy.astype(jnp.float32)
    (
        feat_gain,
        feat_bias,
        proj_bias,
        query_bias,
        value_bias,
        out_bias,
        attn_gain,
        attn_shift,
        hidden_bias,
        down_bias,
        final_gain,
        final_shift,
    ) = vector_pieces(vector)
    rows, length, channels = features.shape
    width = projection_copy.shape[1]
    tokens = rows * length
    head_size = HDIM
    heads = width // head_size
    config = subnet_config[0]
    columns = jnp.arange(width, dtype=jnp.int32)
    keep_width = (columns < config[0]).astype(jnp.float32)
    keep_heads = (columns < config[1] * head_size).astype(jnp.float32)
    keep_hidden = (jnp.arange(feedforward_copy.shape[2], dtype=jnp.int32) < config[2]).astype(
        jnp.float32
    )
    count = config[0].astype(jnp.float32)
    positions = jnp.arange(length, dtype=jnp.int32)
    ends = jnp.cumsum(segment_lengths, axis=1)
    segments = jnp.sum((positions[None, :, None] >= ends[:, None, :]).astype(jnp.int32), -1)

    def middle_norm(value, gain, shift):
        return masked_norm(value, gain, shift, keep_width, count)

    feat_in = features.reshape(tokens, channels).astype(jnp.float32)
    normed, input_pull = jax.vjp(plain_norm, feat_in, feat_gain, feat_bias)
    normed_low = normed.astype(jnp.bfloat16)
    hidden = (
        jnp.dot(normed_low, projection_copy, preferred_element_type=jnp.float32) + proj_bias
    ) * keep_width
    hidden_low = hidden.astype(jnp.bfloat16)
    triple = jnp.einsum(
        "td,kde->kte", hidden_low, attention_copy, preferred_element_type=jnp.float32
    )
    biases = jnp.stack([query_bias, jnp.zeros_like(query_bias), value_bias])
    triple_low = ((triple + biases[:, None, :]) * keep_heads).astype(jnp.bfloat16)
    heads_view = triple_low.reshape(3, rows, length, heads, head_size)
    mixed, totals = lax.map(attend_row, (heads_view[0], heads_view[1], heads_view[2], segments))
    mixed_low = mixed.reshape(tokens, width).astype(jnp.bfloat16)
    branch = (
        jnp.dot(mixed_low, output_copy, preferred_element_type=jnp.float32) + out_bias
    ) * keep_width
    first, first_pull = jax.vjp(middle_norm, hidden + branch, attn_gain, attn_shift)
    first_low = first.astype(jnp.bfloat16)
    inner = (
        jnp.dot(first_low, feedforward_copy[0], preferred_element_type=jnp.float32) + hidden_bias
    ) * keep_hidden
    active, gelu_pull = jax.vjp(exact_gelu, inner)
    active_low = active.astype(jnp.bfloat16)
    down = (
        jnp.einsum("tf,df->td", active_low, feedforward_copy[1], preferred_element_type=jnp.float32)
        + down_bias
    ) * keep_width
    final, final_pull = jax.vjp(middle_norm, first + down, final_gain, final_shift)
    activations = final.astype(jnp.bfloat16).reshape(rows, length, width)
    final_grad = cotangent.reshape(tokens, width).astype(jnp.float32)
    second_grad, final_gain_grad, final_shift_grad = final_pull(final_grad)
    down_grad = (second_grad * keep_width).astype(jnp.bfloat16)
    down_bias_grad = jnp.sum(down_grad.astype(jnp.float32), 0)
    down_matrix_grad = jnp.einsum(
        "td,tf->df", down_grad, active_low, preferred_element_type=jnp.float32
    )
    active_grad = jnp.dot(down_grad, feedforward_copy[1], preferred_element_type=jnp.float32)
    (inner_raw,) = gelu_pull(active_grad)
    inner_grad = (inner_raw * keep_hidden).astype(jnp.bfloat16)
    hidden_bias_grad = jnp.sum(inner_grad.astype(jnp.float32), 0)
    up_matrix_grad = jnp.einsum(
        "td,tf->df", first_low, inner_grad, preferred_element_type=jnp.float32
    )
    first_grad = second_grad + jnp.einsum(
        "tf,df->td", inner_grad, feedforward_copy[0], preferred_element_type=jnp.float32
    )
    first_sum_grad, attn_gain_grad, attn_shift_grad = first_pull(first_grad)
    branch_grad = (first_sum_grad * keep_width).astype(jnp.bfloat16)
    out_bias_grad = jnp.sum(branch_grad.astype(jnp.float32), 0)
    output_grad = jnp.einsum(
        "td,te->de", mixed_low, branch_grad, preferred_element_type=jnp.float32
    )
    mixed_grad = jnp.einsum(
        "te,de->td", branch_grad, output_copy, preferred_element_type=jnp.float32
    ).astype(jnp.bfloat16)
    query_part, key_part, value_part = lax.map(
        attend_back,
        (
            heads_view[0],
            heads_view[1],
            heads_view[2],
            segments,
            mixed_grad.reshape(rows, length, heads, head_size),
            totals,
        ),
    )
    triple_grad = (
        jnp.stack([query_part, key_part, value_part]).reshape(3, tokens, width) * keep_heads
    ).astype(jnp.bfloat16)
    query_bias_grad = jnp.sum(triple_grad[0].astype(jnp.float32), 0)
    value_bias_grad = jnp.sum(triple_grad[2].astype(jnp.float32), 0)
    attention_grad = jnp.einsum(
        "td,kte->kde", hidden_low, triple_grad, preferred_element_type=jnp.float32
    )
    hidden_grad = (
        (
            first_sum_grad
            + jnp.einsum(
                "kte,kde->td", triple_grad, attention_copy, preferred_element_type=jnp.float32
            )
        )
        * keep_width
    ).astype(jnp.bfloat16)
    proj_bias_grad = jnp.sum(hidden_grad.astype(jnp.float32), 0)
    projection_grad = jnp.einsum(
        "tc,td->cd", normed_low, hidden_grad, preferred_element_type=jnp.float32
    )
    normed_grad = jnp.einsum(
        "td,cd->tc", hidden_grad, projection_copy, preferred_element_type=jnp.float32
    )
    feat_grad, feat_gain_grad, feat_bias_grad = input_pull(normed_grad)
    input_gradient = (0.1 * feat_grad).reshape(rows, length, channels)
    small_grad = jnp.concatenate(
        [
            feat_gain_grad,
            feat_bias_grad,
            proj_bias_grad,
            query_bias_grad,
            value_bias_grad,
            out_bias_grad,
            attn_gain_grad,
            attn_shift_grad,
            hidden_bias_grad,
            down_bias_grad,
            final_gain_grad,
            final_shift_grad,
        ]
    )
    feedforward_grad = jnp.stack([up_matrix_grad, down_matrix_grad])
    summed = (
        lax.psum_scatter(projection_grad, ("grp", "dp"), scatter_dimension=0, tiled=True),
        lax.psum_scatter(attention_grad, ("grp", "dp"), scatter_dimension=1, tiled=True),
        lax.psum_scatter(output_grad, ("grp", "dp"), scatter_dimension=0, tiled=True),
        lax.psum_scatter(feedforward_grad, ("grp", "dp"), scatter_dimension=1, tiled=True),
        lax.psum_scatter(small_grad, ("grp", "dp"), scatter_dimension=0, tiled=True),
    )
    proj_m, proj_v, proj_w = adam(
        projection_weight, projection_moment, projection_square, summed[0], RATE
    )
    attn_m, attn_v, attn_w = adam(
        attention_weight, attention_moment, attention_square, summed[1], RATE
    )
    out_m, out_v, out_w = adam(output_weight, output_moment, output_square, summed[2], RATE)
    ffn_m, ffn_v, ffn_w = adam(
        feedforward_weight, feedforward_moment, feedforward_square, summed[3], RATE
    )
    small_m, small_v, small_w = adam(
        small_params, small_moment, small_square, summed[4], SMALL_RATE
    )
    return (
        activations,
        input_gradient,
        summed[0],
        proj_m,
        proj_v,
        proj_w,
        summed[1],
        attn_m,
        attn_v,
        attn_w,
        summed[2],
        out_m,
        out_v,
        out_w,
        summed[3],
        ffn_m,
        ffn_v,
        ffn_w,
        summed[4],
        small_m,
        small_v,
        small_w,
    )


def solution(mesh):
    return jax.shard_map(
        per_device,
        mesh=mesh,
        in_specs=(
            P(("grp", "dp"), None, None),
            P(("grp", "dp"), None),
            P("grp", None),
            P(("grp", "dp"), None, None),
            P(("grp", "dp"), None),
            P(("grp", "dp"), None),
            P(("grp", "dp"), None),
            P(None, ("grp", "dp"), None),
            P(None, ("grp", "dp"), None),
            P(None, ("grp", "dp"), None),
            P(("grp", "dp"), None),
            P(("grp", "dp"), None),
            P(("grp", "dp"), None),
            P(None, ("grp", "dp"), None),
            P(None, ("grp", "dp"), None),
            P(None, ("grp", "dp"), None),
            P(("grp", "dp")),
            P(("grp", "dp")),
            P(("grp", "dp")),
        ),
        out_specs=(
            P(("grp", "dp"), None, None),
            P(("grp", "dp"), None, None),
            P(("grp", "dp"), None),
            P(("grp", "dp"), None),
            P(("grp", "dp"), None),
            P(("grp", "dp"), None),
            P(None, ("grp", "dp"), None),
            P(None, ("grp", "dp"), None),
            P(None, ("grp", "dp"), None),
            P(None, ("grp", "dp"), None),
            P(("grp", "dp"), None),
            P(("grp", "dp"), None),
            P(("grp", "dp"), None),
            P(("grp", "dp"), None),
            P(None, ("grp", "dp"), None),
            P(None, ("grp", "dp"), None),
            P(None, ("grp", "dp"), None),
            P(None, ("grp", "dp"), None),
            P(("grp", "dp")),
            P(("grp", "dp")),
            P(("grp", "dp")),
            P(("grp", "dp")),
        ),
        check_vma=False,
    )
```

profile of v0, /device:TPU:0, one launch (start us, length us, event | category | flops | bytes accessed | tf_op | source)
XLA Modules:
  0.0 1191.6 jit_solution(10450700737373110568)
XLA Ops:
  16.1 42.4 %all-reduce = bf16[11008]{0:T(1024)(128)(2,1)S(1)} all-reduce(bf16[11008]{0:T(1024)(128)(2,1)S(1)} %dynamic-update-slice), channel_id=1, replica_groups=mesh['grp'=4,'dp'=8] {'grp','dp'}, use_global_device_ids=true, to_apply=%add | all-reduce | flops 11008 | bytes 44032
  69.1 43.6 %all_gather.16 = bf16[512,768]{1,0:T(8,128)(2,1)S(1)} all-gather(bf16[16,768]{1,0:T(8,128)(2,1)S(1)} %convert_element_type.157), channel_id=1, replica_groups=mesh['grp'=4,'dp'=8] {'grp','dp'}, dimensions={0}, use_global_device_ids=true | all-gather | bytes 811008 | tf_op jit(solution)/shard_map/all_gather | solution.py:140
  124.3 11.2 fusion.7
  135.6 12.0 %fusion.6 = (f32[12,512]{1,0:T(8,128)S(1)}, f32[12,512,1024]{2,1,0:T(8,128)}) fusion(pred[512,1024]{1,0:T(8,128)(4,1)S(1)} %get-tuple-element.218, bf16[512,12,64]{0,2,1:T(8,128)(2,1)S(1)} %bitcast.167, bf16[1024,12,64]{0,2,1:T(8,128)(2,1)S(1)} %bitcast.157), kind=kOutput, calls=%fused_computation.20 | convolution fusion | flops 824174592 | bytes 28073984 | tf_op jit(solution)/shard_map/while/body/eval_jaxpr/qhd,khd->hqk/dot_general | solution.py:62
  147.6 21.6 %fusion.4 = (f32[12,512]{1,0:T(8,128)S(1)}, f32[12,512]{1,0:T(8,128)S(1)}) fusion(f32[12,512,1024]{2,1,0:T(8,128)} %get-tuple-element.228, f32[12,512]{1,0:T(8,128)S(1)} %get-tuple-element.227, pred[512,1024]{1,0:T(8,128)(4,1)S(1)} %get-tuple-element.218, f32[12,512]{1,0:T(8,128)S(1)} %get-tuple-element.225, f32[12,512,1024]{2,1,0:T(8,128)} %get-tuple-element.226, ...), kind=kLoop, calls=%fused_computation.16 | loop fusion | flops 50319360 | bytes 51478528 | tf_op jit(solution)/shard_map/while/body/eval_jaxpr/reduce_sum | solution.py:66
  177.1 13.2 %fusion.82 = bf16[512,12,64]{0,2,1:T(8,128)(2,1)S(1)} fusion(bf16[1024,12,64]{0,2,1:T(8,128)(2,1)S(1)} %bitcast.153, f32[12,512,1024]{2,1,0:T(8,128)} %get-tuple-element.228, f32[12,512]{1,0:T(8,128)S(1)} %get-tuple-element.240, f32[12,512]{1,0:T(8,128)S(1)} %get-tuple-element.227, pred[512,1024]{1,0:T(8,128)(4,1)S(1)} %get-tuple-element.218), kind=kOutput, calls=%fused_computation.129 | convolution fusion | flops 837156864 | bytes 28098560 | tf_op jit(solution)/shard_map/while/body/eval_jaxpr/hqk,khd->qhd/dot_general | solution.py:69
  198.6 18.0 %all-gather.8.cloned.1.call-done = bf16[2,768,3072]{2,1,0:T(8,128)(2,1)} async-done(((bf16[2,24,3072]{2,1,0:T(8,128)(2,1)}), bf16[2,768,3072]{2,1,0:T(8,128)(2,1)}) %all-gather.8.cloned.1.call-update) | async-done | bytes 9437200 | tf_op jit(solution)/shard_map/all_gather | solution.py:143
  216.6 39.4 %multiply_convert_fusion.3 = (bf16[1024,3072]{1,0:T(8,128)(2,1)S(1)}, f32[1024,3072]{1,0:T(8,128)}, f32[1024,3072]{1,0:T(8,128)}) fusion(f32[3072]{0:T(1024)S(1)} %copy-done.64, f32[3072]{0:T(1024)S(1)} %copy-done.63, bf16[2,768,3072]{2,1,0:T(8,128)(2,1)} %all-gather.8.cloned.1.call-done, f32[768]{0:T(1024)S(1)} %copy-done.65, f32[768]{0:T(1024)S(1)} %copy-done.52, ...), kind=kOutput, calls=%fused_computation.29 | convolution fusion | flops 5048107008 | bytes 39363584 | tf_op jit(solution)/shard_map/dot_general | solution.py:202
  272.5 19.9 %convert_reduce_fusion = (f32[3072]{0:T(1024)}, bf16[1024,3072]{1,0:T(8,128)(2,1)}) fusion(f32[1024,3072]{1,0:T(8,128)} %get-tuple-element.199, bf16[1024,768]{0,1:T(8,128)(2,1)S(1)} %get-tuple-element.178, bf16[2,768,3072]{2,1,0:T(8,128)(2,1)} %all-gather.8.cloned.1.call-done, f32[3072]{0:T(1024)S(1)} %copy-done.64, f32[1024,3072]{1,0:T(8,128)} %get-tuple-element.231, ...), kind=kOutput, calls=%fused_computation.23 | convolution fusion | flops 4891603968 | bytes 37785600 | tf_op jit(solution)/shard_map/dot_general | solution.py:219
  292.4 10.7 multiply_reduce_fusion.2
  309.6 10.1 fusion.150
  319.7 48.7 %fusion.77 = f32[512,12,64]{0,2,1:T(8,128)} fusion(bf16[1024,12,64]{0,2,1:T(8,128)(2,1)S(1)} %bitcast.158, f32[12,512,1024]{2,1,0:T(8,128)} %fusion.150, pred[512,1024]{1,0:T(8,128)(4,1)} %copy-done.18, f32[12,512]{1,0:T(8,128)S(1)} %copy-done.48, f32[12,512,1024]{2,1,0:T(8,128)} %get-tuple-element.228), kind=kOutput, calls=%fused_computation.126 | convolution fusion | flops 880811008 | bytes 54026240 | tf_op jit(solution)/shard_map/while/body/eval_jaxpr/hqk,khd->qhd/dot_general | solution.py:98
  368.4 50.3 %fusion.24 = f32[12,64,1024]{2,1,0:T(8,128)} fusion(bf16[512,12,64]{0,2,1:T(8,128)(2,1)} %bitcast.168, f32[12,512,1024]{2,1,0:T(8,128)} %fusion.150, pred[512,1024]{1,0:T(8,128)(4,1)} %copy-done.18, f32[12,512]{1,0:T(8,128)S(1)} %copy-done.48, f32[12,512,1024]{2,1,0:T(8,128)} %get-tuple-element.228), kind=kOutput, calls=%fused_computation.49 | convolution fusion | flops 880811008 | bytes 54812672 | tf_op jit(solution)/shard_map/while/body/eval_jaxpr/hqk,qhd->khd/dot_general | solution.py:100
  418.7 11.7 fusion.151
  430.5 11.5 fusion.9
  442.0 13.5 %fusion.69 = f32[12,64,1024]{2,1,0:T(8,128)} fusion(f32[12,64,1024]{2,1,0:T(8,128)S(1)} %fusion.9, bf16[512,12,64]{0,2,1:T(8,128)(2,1)S(1)} %bitcast.162, f32[12,512]{1,0:T(8,128)S(1)} %copy-done.48, f32[12,512,1024]{2,1,0:T(8,128)} %get-tuple-element.228, pred[512,1024]{1,0:T(8,128)(4,1)S(1)} %copy-done.19), kind=kOutput, calls=%fused_computation.120 | convolution fusion | flops 831258624 | bytes 32792576 | tf_op jit(solution)/shard_map/while/body/eval_jaxpr/hqk,qhd->khd/dot_general | solution.py:103
  455.5 49.3 %fusion.74 = f32[512,12,64]{0,2,1:T(8,128)} fusion(bf16[1024,12,64]{0,2,1:T(8,128)(2,1)S(1)} %bitcast.159, f32[12,512,1024]{2,1,0:T(8,128)} %fusion.151, pred[512,1024]{1,0:T(8,128)(4,1)} %copy-done.16, f32[12,512]{1,0:T(8,128)S(1)} %copy-done.47, f32[12,512,1024]{2,1,0:T(8,128)} %get-tuple-element.226), kind=kOutput, calls=%fused_computation.125 | convolution fusion | flops 880811008 | bytes 54026240 | tf_op jit(solution)/shard_map/while/body/eval_jaxpr/hqk,khd->qhd/dot_general | solution.py:98
  504.9 54.2 %fusion.66 = f32[12,64,1024]{2,1,0:T(8,128)} fusion(f32[12,64,1024]{2,1,0:T(8,128)} %fusion.24, bf16[512,12,64]{0,2,1:T(8,128)(2,1)S(1)} %bitcast.166, f32[12,512,1024]{2,1,0:T(8,128)} %fusion.151, pred[512,1024]{1,0:T(8,128)(4,1)} %copy-done.16, f32[12,512]{1,0:T(8,128)S(1)} %copy-done.47, f32[12,512,1024]{2,1,0:T(8,128)} %get-tuple-element.226), kind=kOutput, calls=%fused_computation.119 | convolution fusion | flops 881597440 | bytes 57958400 | tf_op jit(solution)/shard_map/while/body/eval_jaxpr/hqk,qhd->khd/dot_general | solution.py:100
  577.6 10.2 convolution_bitcast_fusion.2
  587.9 11.1 copy.98
  647.4 39.9 %all-reduce.2 = f32[11008]{0:T(1024)S(1)} all-reduce(f32[11008]{0:T(1024)} %constant_dynamic-update-slice_fusion), channel_id=6, replica_groups=mesh['grp'=4,'dp'=8] {'grp','dp'}, use_global_device_ids=true, to_apply=%region_36.37.clone | all-reduce | flops 11008 | bytes 88064
  692.3 80.5 %reduce-scatter.6.cloned.1.call-done = f32[24,768]{1,0:T(8,128)} async-done(((f32[768,768]{1,0:T(8,128)}), f32[24,768]{1,0:T(8,128)}) %reduce-scatter.6.cloned.1.call-update) | async-done | bytes 73744 | tf_op jit(solution)/shard_map/reduce_scatter | solution.py:295
  774.4 194.9 %all-reduce.5.cloned.1.call-done = f32[3,768,768]{2,0,1:T(4,128)} async-done(((f32[3,768,768]{2,0,1:T(4,128)}), f32[3,768,768]{2,0,1:T(4,128)}) %all-reduce.5.cloned.1.call-update) | async-done | bytes 7077904
  972.4 209.1 %reduce-scatter.8.cloned.1.call-done = f32[2,24,3072]{2,1,0:T(8,128)} async-done(((f32[2,768,3072]{2,1,0:T(8,128)}), f32[2,24,3072]{2,1,0:T(8,128)}) %reduce-scatter.8.cloned.1.call-update) | async-done | bytes 589840 | tf_op jit(solution)/shard_map/reduce_scatter | solution.py:296
  (274 shorter events, 147.9 us)
Async XLA Ops:
  7.2 106.4 %copy-start.2 = (bf16[1,1024,512]{2,1,0:T(8,128)(2,1)S(1)}, bf16[1,1024,512]{2,1,0:T(8,128)(2,1)}, u32[]{:S(2)}) copy-start(bf16[1,1024,512]{2,1,0:T(8,128)(2,1)} %param.19) | copy-start | bytes 3145732
  7.2 58.7 %copy-start.25 = (bf16[1,1024,768]{2,1,0:T(8,128)(2,1)S(1)}, bf16[1,1024,768]{2,1,0:T(8,128)(2,1)}, u32[]{:S(2)}) copy-start(bf16[1,1024,768]{2,1,0:T(8,128)(2,1)} %param.22) | copy-start | bytes 4718596
  7.2 109.4 %all-gather.4.cloned.1.call-start = ((), (), s32[]{:S(2)}) async-start(), calls=%async_computation.3 | async-start | bytes 3649536 | tf_op jit(solution)/shard_map/all_gather | solution.py:141
  9.0 182.6 %all-gather.6.cloned.1.call-start = ((), (), s32[]{:S(2)}) async-start(), calls=%async_computation.4 | async-start | bytes 1216512 | tf_op jit(solution)/shard_map/all_gather | solution.py:142
  10.6 205.9 %all-gather.8.cloned.1.call-start = ((), (), s32[]{:S(2)}) async-start(), calls=%async_computation.5 | async-start | bytes 9732096 | tf_op jit(solution)/shard_map/all_gather | solution.py:143
  12.5 678.3 %reduce-scatter.4.cloned.1.call-start = ((), (), s32[]{:S(2)}) async-start(), calls=%async_computation.6 | async-start | bytes 1622016 | tf_op jit(solution)/shard_map/reduce_scatter | solution.py:293
  59.7 131.9 %copy-start.67 = (f32[768]{0:T(1024)}, f32[768]{0:T(1024)S(1)}, u32[]{:S(2)}) copy-start(f32[768]{0:T(1024)S(1)} %get-tuple-element.211) | copy-start | bytes 9220
  62.1 54.5 %copy-start.35 = (f32[1024]{0:T(1024)}, f32[1024]{0:T(1024)S(1)}, u32[]{:S(2)}) copy-start(f32[1024]{0:T(1024)S(1)} %broadcast_multiply_fusion) | copy-start | bytes 12292
  63.8 52.7 %copy-start.43 = (f32[1024]{0:T(1024)}, f32[1024]{0:T(1024)S(1)}, u32[]{:S(2)}) copy-start(f32[1024]{0:T(1024)S(1)} %fusion.64) | copy-start | bytes 12292
  68.3 55.5 %copy-start.72 = (f32[512]{0:T(512)}, f32[512]{0:T(512)S(1)}, u32[]{:S(2)}) copy-start(f32[512]{0:T(512)S(1)} %get-tuple-element.217) | copy-start | bytes 6148
  69.1 100.0 %copy-start.16 = (pred[512,1024]{1,0:T(8,128)(4,1)}, pred[512,1024]{1,0:T(8,128)(4,1)S(1)}, u32[]{:S(2)}) copy-start(pred[512,1024]{1,0:T(8,128)(4,1)S(1)} %get-tuple-element.219) | copy-start | bytes 1572868
  69.1 108.0 %copy-start.18 = (pred[512,1024]{1,0:T(8,128)(4,1)}, pred[512,1024]{1,0:T(8,128)(4,1)S(1)}, u32[]{:S(2)}) copy-start(pred[512,1024]{1,0:T(8,128)(4,1)S(1)} %get-tuple-element.218) | copy-start | bytes 1572868
  124.3 52.8 %copy-start = (bf16[1,1024,768]{1,2,0:T(8,128)(2,1)}, bf16[1,1024,768]{1,2,0:T(8,128)(2,1)S(1)}, u32[]{:S(2)}) copy-start(bf16[1,1024,768]{1,2,0:T(8,128)(2,1)S(1)} %get-tuple-element.203) | copy-start | bytes 4718596
  196.3 106.7 %copy-start.8 = (f32[1024,768]{0,1:T(8,128)}, f32[1024,768]{0,1:T(8,128)S(1)}, u32[]{:S(2)}) copy-start(f32[1024,768]{0,1:T(8,128)S(1)} %get-tuple-element.230) | copy-start | bytes 9437188
  196.4 106.7 %copy-start.41 = (f32[1024]{0:T(1024)}, f32[1024]{0:T(1024)S(1)}, u32[]{:S(2)}) copy-start(f32[1024]{0:T(1024)S(1)} %broadcast_divide_fusion.1) | copy-start | bytes 12292
  196.9 106.2 %copy-start.54 = (f32[1024]{0:T(1024)}, f32[1024]{0:T(1024)S(1)}, u32[]{:S(2)}) copy-start(f32[1024]{0:T(1024)S(1)} %fusion.95) | copy-start | bytes 12292
  455.5 49.3 %copy-start.21 = (bf16[1,512,768]{1,2,0:T(8,128)(2,1)S(1)}, bf16[1,512,768]{1,2,0:T(8,128)(2,1)}, u32[]{:S(2)}) copy-start(bf16[1,512,768]{1,2,0:T(8,128)(2,1)} %copy-done.20) | copy-start | bytes 2359300
  504.9 54.2 %copy-start.30 = (f32[512,12,64]{0,2,1:T(8,128)S(1)}, f32[512,12,64]{0,2,1:T(8,128)}, u32[]{:S(2)}) copy-start(f32[512,12,64]{0,2,1:T(8,128)} %fusion.77) | copy-start | bytes 4718596
  573.3 199.5 %reduce-scatter.6.cloned.1.call-start = ((), (), s32[]{:S(2)}) async-start(), calls=%async_computation.7 | async-start | bytes 2433024 | tf_op jit(solution)/shard_map/reduce_scatter | solution.py:295
  577.6 391.8 %all-reduce.5.cloned.1.call-start = ((), (), s32[]{:S(2)}) async-start(), calls=%async_computation.9 | async-start | bytes 18874368
  599.1 582.4 %reduce-scatter.8.cloned.1.call-start = ((), (), s32[]{:S(2)}) async-start(), calls=%async_computation.8 | async-start | bytes 19464192 | tf_op jit(solution)/shard_map/reduce_scatter | solution.py:296
  630.0 60.7 %copy-start.34 = (f32[16,768]{1,0:T(8,128)S(1)}, f32[16,768]{1,0:T(8,128)}, u32[]{:S(2)}) copy-start(f32[16,768]{1,0:T(8,128)} %param.23) | copy-start | bytes 147460
  630.0 142.7 %copy-start.33 = (f32[24,768]{1,0:T(8,128)S(1)}, f32[24,768]{1,0:T(8,128)}, u32[]{:S(2)}) copy-start(f32[24,768]{1,0:T(8,128)} %param.29) | copy-start | bytes 221188
  634.0 336.4 %copy-start.31 = (f32[3,24,768]{2,1,0:T(8,128)S(1)}, f32[3,24,768]{2,1,0:T(8,128)}, u32[]{:S(2)}) copy-start(f32[3,24,768]{2,1,0:T(8,128)} %param.26) | copy-start | bytes 663556
  (67 other events, 844.6 us)
Sparse Core Ops, SparseCore 0:
  11.8 63.2 all-gather.3
  78.6 53.0 all-gather.5
  135.5 81.0 all-gather.7
  573.4 95.6 reduce-scatter.3
  674.7 97.9 reduce-scatter.5
  779.4 189.9 all-reduce.4
  976.3 205.0 reduce-scatter.7
where the time goes:
time: 1200 us; the launch traced here: 1190 us
  waiting for transfers between devices  503 us (42%)
  matrix products  429 us (36%)
  blocking collectives  126 us (10%)
  other arithmetic  73.1 us (6%)
  local copies, waits for them, and re-layouts  43.9 us (4%)
  between operations  16.8 us (1%)
    reduce_scatter x1, waiting for transfers between devices, per_device(): lax.psum_scatter(feedforward_grad, ('grp', 'dp'), scatter_dimension=1, ti...  209 us
    unnamed x8, waiting for transfers between devices  195 us
    dot_general x2, matrix products, attend_back(): jnp.einsum('hqk,qhd->khd', raw_grad, block_query, preferred_element_type=...  105 us
    dot_general x2, matrix products, attend_back(): jnp.einsum('hqk,khd->qhd', raw_grad, key, preferred_element_type=jnp.floa...  98 us
    unnamed x2, blocking collectives  82.3 us
    reduce_scatter x1, waiting for transfers between devices, per_device(): lax.psum_scatter(output_grad, ('grp', 'dp'), scatter_dimension=0, tiled=T...  80.5 us
    all_gather x1, blocking collectives, per_device(): lax.all_gather(projection_weight.astype(jnp.bfloat16), ('grp', 'dp'), axi...  43.6 us
    dot_general x1, matrix products, per_device(): jnp.dot(first_low, feedforward_copy[0], preferred_element_type=jnp.float32)  39.4 us
  transfers between devices with their start and end apart: 7, of which 4 were waited for; matrix products, arithmetic and copies ran while one was open for 15% of the time, Pallas kernels for 0%

commit v1 on v0

v1 whole, which is shorter than its diff:
```python
import functools
import math

import jax
import jax.numpy as jnp
from jax import lax
from jax.experimental import pallas as pl
from jax.experimental.pallas import tpu as pltpu
from jax.sharding import PartitionSpec as P

D = 768
FF = 3072
FEAT = 512
HDIM = 64
HEADS = 12
PAIRS = HEADS // 2
LEN = 1024
STEP = 10
TILE = 256
NT = LEN // TILE
VEC = 11008

NORM_EPS = 1e-05
RATE = 0.08
SMALL_RATE = 0.3
BETA_ONE = 0.9
BETA_TWO = 0.999
ADAM_EPS = 1e-08
DECAY = 0.01

F32 = jnp.float32
BF16 = jnp.bfloat16
BIG = 2.0**100
VMEM_LIMIT = 63 << 20

WIDTHS = dict(
    g0=FEAT, b0=FEAT, bp=D, bq=D, bv=D, bo=D, g1=D, c1=D, b1=FF, b2=D, g2=D, c2=D
)
OFFSETS = {}
_at = 0
for _name, _width in WIDTHS.items():
    OFFSETS[_name] = _at
    _at += _width

KEY_RANGE = [
    (max(0, (i * TILE - 511) // TILE * TILE), min(LEN, -(-(i * TILE + TILE + 511) // TILE) * TILE))
    for i in range(NT)
]


def mm(a, b):
    return jnp.dot(a, b, preferred_element_type=F32)


def mm_nt(a, b):
    return lax.dot_general(a, b, (((1,), (1,)), ((), ())), preferred_element_type=F32)


def piece(ref, name, start=0, width=None):
    begin = OFFSETS[name] + start
    return ref[0:1, begin : begin + (width or WIDTHS[name])]


def put(ref, name, value, start=0):
    begin = OFFSETS[name] + start
    ref[0:1, begin : begin + value.shape[1]] = value


def keep_row(width, limit, start=0):
    lane = lax.broadcasted_iota(jnp.int32, (1, width), 1) + start
    return (lane < limit).astype(F32)


def col_sum(value):
    return jnp.sum(value, 0, keepdims=True)


def row_sum(value):
    return jnp.sum(value, 1, keepdims=True)


def rows_of(t):
    return pl.ds(pl.multiple_of(t * TILE, TILE), TILE)


def lanes_of(p, width=128):
    return pl.ds(pl.multiple_of(p * width, width), width)


def gelu_both(u):
    half = jnp.exp(-0.5 * u * u)
    t = 1.0 / (1.0 + (0.3275911 * 0.7071067811865476) * jnp.abs(u))
    poly = 0.5 * 1.061405429
    for c in (-1.453152027, 1.421413741, -0.284496736, 0.254829592):
        poly = poly * t + 0.5 * c
    tail = poly * t * half
    cdf = jnp.where(u >= 0.0, 1.0 - tail, tail)
    return u * cdf, cdf + u * (half * 0.3989422804014327)


def fill_patterns(seg_ref, kpat, qpat):
    e0 = seg_ref[0, 0]
    e1 = e0 + seg_ref[0, 1]
    e2 = e1 + seg_ref[0, 2]

    @pl.loop(0, NT)
    def _(t):
        pos = lax.broadcasted_iota(jnp.int32, (TILE, 128), 0) + t * TILE
        lane = lax.broadcasted_iota(jnp.int32, (TILE, 128), 1)
        seg = (
            (pos >= e0).astype(jnp.int32)
            + (pos >= e1).astype(jnp.int32)
            + (pos >= e2).astype(jnp.int32)
        )
        for e in range(2):
            slot = lane - (64 if e == 0 else 0)
            valid = (slot >= 0) & (slot < 4)
            same = slot == seg
            kpat[e, rows_of(t), :] = jnp.where(same, 1.0, 0.0).astype(BF16)
            qpat[e, rows_of(t), :] = jnp.where(valid & (slot != seg), -BIG, 0.0).astype(BF16)


def half_mask(e):
    lane = lax.broadcasted_iota(jnp.int32, (1, 128), 1)
    return ((lane < 64) if e == 0 else (lane >= 64)).astype(F32).astype(BF16)


def norm0(feat, svec, rows):
    x = feat[rows, :].astype(F32)
    centred = x - row_sum(x) * (1.0 / FEAT)
    inv = lax.rsqrt(row_sum(centred * centred) * (1.0 / FEAT) + NORM_EPS)
    hat = centred * inv
    normed = (hat * piece(svec, "g0") + piece(svec, "b0")).astype(BF16)
    return hat, inv, normed


def forward_kernel(
    upto,
    seg_ref, cfg_ref, feat_hbm, cot_hbm, wg_hbm, wp_hbm, svec_in,
    act_out, hl_out, hlt_out, qkv_out, kt_out, mixed_out, mixedt_out, xh1_out, inv1_out, flt_out,
    active_out, gp_out, d2_out, dg_out, dgt_out, lse_out, sg_out,
    feat, cot, wg, wp, hid, hl, hlt, qkv, kt, vt, mixed, mixedt, xh1, fl, flt, active, gp, dg, dgt, act,
    kpat, qpat, sem_in, sem_out,
):
    svec = svec_in
    outs = []

    def load(i, src, dst):
        copy = pltpu.make_async_copy(src, dst, sem_in.at[i])
        copy.start()
        return copy

    def save(src, dst):
        copy = pltpu.make_async_copy(src, dst, sem_out.at[len(outs)])
        copy.start()
        outs.append(copy)

    c_feat = load(0, feat_hbm, feat)
    c_wp = load(1, wp_hbm, wp)
    c_w = [load(2 + u, wg_hbm.at[u], wg.at[u]) for u in range(12)]
    c_cot = load(14, cot_hbm, cot)

    width = cfg_ref[0, 0]
    count = 1.0 / width.astype(F32)
    fill_patterns(seg_ref, kpat, qpat)
    c_feat.wait()
    c_wp.wait()

    @pl.loop(0, NT)
    def _(t):
        rows = rows_of(t)
        normed = norm0(feat, svec, rows)[2]
        h = (mm(normed, wp[...]) + piece(svec, "bp")) * keep_row(D, width)
        hid[rows, :] = h
        low = h.astype(BF16)
        hl[rows, :] = low
        hlt[:, rows] = low.T

    save(hl, hl_out)
    save(hlt, hlt_out)
    for u in range(3):
        c_w[u].wait()

    @pl.loop(0, NT)
    def _(t):
        rows = rows_of(t)
        keep = keep_row(D, cfg_ref[0, 1] * HDIM)
        low = hl[rows, :]
        qkv[0, rows, :] = ((mm(low, wg[0]) + piece(svec, "bq")) * keep).astype(BF16)
        k = (mm(low, wg[1]) * keep).astype(BF16)
        qkv[1, rows, :] = k
        kt[:, rows] = k.T
        v = ((mm(low, wg[2]) + piece(svec, "bv")) * keep).astype(BF16)
        qkv[2, rows, :] = v
        vt[:, rows] = v.T

    save(qkv, qkv_out)
    save(kt, kt_out)

    if upto >= 2:

        @pl.loop(0, PAIRS)
        def _(p):
            lanes = lanes_of(p)
            for e in range(2):
                kaug = qkv[1, :, lanes] * half_mask(e) + kpat[e]
                head_rows = pl.ds(pl.multiple_of(p * 128 + 64 * e, 64), 64)
                for b in range(NT):
                    lo, hi = KEY_RANGE[b]
                    cols = slice(b * TILE, (b + 1) * TILE)
                    qaug = qkv[0, cols, lanes] * (half_mask(e) * 0.125) + qpat[e, cols, :]
                    st = mm_nt(kaug[lo:hi], qaug)
                    peak = jnp.max(st, 0, keepdims=True)
                    power = jnp.exp(st - peak)
                    total = col_sum(power)
                    ot = mm(vt[head_rows, lo:hi], power.astype(BF16))
                    mixedt[head_rows, cols] = (ot * (1.0 / total)).astype(BF16)
                    lse_out[pl.ds(2 * p + e, 1), cols] = peak + jnp.log(total)

    save(mixedt, mixedt_out)
    c_w[3].wait()

    if upto >= 3:

        @pl.loop(0, NT)
        def _(t):
            rows = rows_of(t)
            keep = keep_row(D, width)
            mix = mixedt[:, rows].T
            mixed[rows, :] = mix
            z = hid[rows, :] + (mm(mix, wg[3]) + piece(svec, "bo")) * keep
            centred = (z - row_sum(z * keep) * count) * keep
            inv = lax.rsqrt(row_sum(centred * centred) * count + NORM_EPS)
            hat = centred * inv
            first = (hat * piece(svec, "g1") + piece(svec, "c1")) * keep
            xh1[rows, :] = hat.astype(BF16)
            inv1_out[rows, :] = jnp.broadcast_to(inv, (TILE, 128))
            hid[rows, :] = first + piece(svec, "b2") * keep
            low = first.astype(BF16)
            fl[rows, :] = low
            flt[:, rows] = low.T

    save(mixed, mixed_out)
    save(xh1, xh1_out)
    save(flt, flt_out)

    if upto >= 4:
        for q in range(4):
            c_w[4 + q].wait()
            c_w[8 + q].wait()

            @pl.loop(0, NT)
            def _(t, q=q):
                rows = rows_of(t)
                u = (mm(fl[rows, :], wg[4 + q]) + piece(svec, "b1", q * D, D)) * keep_row(
                    D, cfg_ref[0, 2], q * D
                )
                g, slope = gelu_both(u)
                low = g.astype(BF16)
                active[q, rows, :] = low
                gp[q, rows, :] = slope.astype(BF16)
                hid[rows, :] += mm_nt(low, wg[8 + q]) * keep_row(D, width)

            save(active.at[q], active_out.at[q])
            save(gp.at[q], gp_out.at[q])
    c_cot.wait()
    if upto < 4:
        for q in range(8):
            c_w[4 + q].wait()

    zero = jnp.zeros((1, D), F32)

    def last(t, sums):
        gain_sum, shift_sum, bias_sum = sums
        rows = rows_of(t)
        keep = keep_row(D, width)
        z = hid[rows, :]
        centred = (z - row_sum(z * keep) * count) * keep
        inv = lax.rsqrt(row_sum(centred * centred) * count + NORM_EPS)
        hat = centred * inv
        gain = piece(svec, "g2")
        act[rows, :] = ((hat * gain + piece(svec, "c2")) * keep).astype(BF16)
        g = cot[rows, :].astype(F32) * keep
        gain_sum = gain_sum + col_sum(g * hat)
        shift_sum = shift_sum + col_sum(g)
        a = g * gain
        d2 = inv * (a - keep * (row_sum(a) * count) - hat * (row_sum(a * hat) * count))
        hid[rows, :] = d2
        low = d2.astype(BF16)
        dg[rows, :] = low
        dgt[:, rows] = low.T
        return gain_sum, shift_sum, bias_sum + col_sum(low.astype(F32))

    gain_sum, shift_sum, bias_sum = lax.fori_loop(0, NT, last, (zero, zero, zero))
    sg_out[...] = jnp.zeros((1, VEC), F32)
    put(sg_out, "g2", gain_sum)
    put(sg_out, "c2", shift_sum)
    put(sg_out, "b2", bias_sum)
    save(act, act_out)
    save(hid, d2_out)
    save(dg, dg_out)
    save(dgt, dgt_out)
    for copy in outs:
        copy.wait()


def backward_kernel(
    upto,
    seg_ref, cfg_ref, feat_hbm, wg_hbm, wp_hbm, svec,
    hlt_hbm, qkv_hbm, kt_hbm, mixed_hbm, mixedt_hbm, xh1_hbm, inv1_hbm, flt_hbm,
    active_hbm, gp_hbm, d2_hbm, dg_hbm, dgt_hbm, lse, sg_in,
    dx_out, gu_out, gwp_out, sg,
    feat, w2q, w1q, wo, wa, wp, hlt, qkv, kt, mixed, mixedt, xh1, inv1, flt, actq, gpq, ig, fg, dg, dgt,
    go, tg, delta, dqt, pbuf, dsbuf, gslot, dxs, kpat, qpat, nrmt, sem_in, sem_q, sem_g, sem_dx,
):
    def load(i, src, dst):
        copy = pltpu.make_async_copy(src, dst, sem_in.at[i])
        copy.start()
        return copy

    n_put = [0]

    def slot_wait(i):
        pltpu.make_async_copy(gslot.at[i], gu_out.at[0], sem_g.at[i]).wait()

    def new_slot():
        i = n_put[0] % 2
        if n_put[0] >= 2:
            slot_wait(i)
        return i

    def send_slot(i, dst):
        pltpu.make_async_copy(gslot.at[i], dst, sem_g.at[i]).start()
        n_put[0] += 1

    def quarter(q):
        s = q % 2
        copies = [
            pltpu.make_async_copy(src, dst, sem_q.at[s, i])
            for i, (src, dst) in enumerate(
                [
                    (active_hbm.at[q], actq.at[s]),
                    (wg_hbm.at[8 + q], w2q.at[s]),
                    (gp_hbm.at[q], gpq.at[s]),
                    (wg_hbm.at[4 + q], w1q.at[s]),
                ]
            )
        ]
        return copies

    c_dgt = load(0, dgt_hbm, dgt)
    for copy in quarter(0):
        copy.start()
    c_dg = load(1, dg_hbm, dg)
    c_flt = load(2, flt_hbm, flt)
    c_d2 = load(3, d2_hbm, fg)
    for copy in quarter(1):
        copy.start()
    c_xh1 = load(4, xh1_hbm, xh1)
    c_inv1 = load(5, inv1_hbm, inv1)
    c_mixed = load(6, mixed_hbm, mixed)
    c_mixedt = load(7, mixedt_hbm, mixedt)
    c_wo = load(8, wg_hbm.at[3], wo)
    c_qkv = load(9, qkv_hbm, qkv)
    c_kt = load(10, kt_hbm, kt)
    c_hlt = load(11, hlt_hbm, hlt)
    c_wa = [load(12 + i, wg_hbm.at[i], wa.at[i]) for i in range(3)]
    c_wp = load(15, wp_hbm, wp)
    c_feat = load(16, feat_hbm, feat)

    width = cfg_ref[0, 0]
    count = 1.0 / width.astype(F32)
    sg[...] = sg_in[...]
    fill_patterns(seg_ref, kpat, qpat)

    def weight_grad(left, right, dst, steps=D // TILE):
        @pl.loop(0, steps)
        def _(m):
            rows = rows_of(m)
            dst[rows, :] = mm(left[rows, :], right[...])

    c_dgt.wait()
    for q in range(4):
        s = q % 2
        copies = quarter(q)
        copies[0].wait()
        i = new_slot()
        weight_grad(dgt, actq.at[s], gslot.at[i])
        send_slot(i, gu_out.at[8 + q])
        if q == 0:
            c_dg.wait()
        copies[1].wait()
        copies[2].wait()

        def inner(t, bias, q=q, s=s):
            rows = rows_of(t)
            low = (
                mm(dg[rows, :], w2q[s])
                * gpq[s, rows, :].astype(F32)
                * keep_row(D, cfg_ref[0, 2], q * D)
            ).astype(BF16)
            ig[rows, :] = low
            return bias + col_sum(low.astype(F32))

        put(sg, "b1", lax.fori_loop(0, NT, inner, jnp.zeros((1, D), F32)), q * D)
        if q == 0:
            c_flt.wait()
            c_d2.wait()
        copies[3].wait()
        i = new_slot()
        weight_grad(flt, ig, gslot.at[i])
        send_slot(i, gu_out.at[4 + q])

        @pl.loop(0, NT)
        def _(t, s=s):
            rows = rows_of(t)
            fg[rows, :] += mm_nt(ig[rows, :], w1q[s])

        if q < 2:
            for copy in quarter(q + 2):
                copy.start()

    for copy in (c_xh1, c_inv1, c_mixed, c_mixedt, c_wo):
        copy.wait()
    zero = jnp.zeros((1, D), F32)

    def middle(t, sums):
        gain_sum, shift_sum, bias_sum = sums
        rows = rows_of(t)
        keep = keep_row(D, width)
        hat = xh1[rows, :].astype(F32)
        g = fg[rows, :] * keep
        gain_sum = gain_sum + col_sum(g * hat)
        shift_sum = shift_sum + col_sum(g)
        a = g * piece(svec, "g1")
        d1 = inv1[rows, 0:1] * (a - keep * (row_sum(a) * count) - hat * (row_sum(a * hat) * count))
        fg[rows, :] = d1
        low = d1.astype(BF16)
        dg[rows, :] = low
        mg = mm_nt(low, wo[...]).astype(BF16)
        go[rows, :] = mg
        product = mg.astype(F32) * mixed[rows, :].astype(F32)
        high = product.astype(BF16)
        rest = (product - high.astype(F32)).astype(BF16)
        lane = lax.broadcasted_iota(jnp.int32, (16, D), 1)
        head = lax.broadcasted_iota(jnp.int32, (16, D), 0)
        pick = ((lane >= head * HDIM) & (lane < head * HDIM + HDIM)).astype(F32).astype(BF16)
        delta[:, rows] = mm_nt(pick, high) + mm_nt(pick, rest)
        return gain_sum, shift_sum, bias_sum + col_sum(low.astype(F32))

    gain_sum, shift_sum, bias_sum = lax.fori_loop(0, NT, middle, (zero, zero, zero))
    put(sg, "g1", gain_sum)
    put(sg, "c1", shift_sum)
    put(sg, "bo", bias_sum)
    i = new_slot()
    weight_grad(mixedt, dg, gslot.at[i])
    send_slot(i, gu_out.at[3])

    c_qkv.wait()
    c_kt.wait()
    c_hlt.wait()
    for copy in c_wa:
        copy.wait()
    for j in range(3):
        if upto >= 2:

            @pl.loop(0, 2)
            def _(pp, j=j):
                p = j * 2 + pp
                lanes = lanes_of(p)
                vpair = qkv[2, :, lanes]
                for e in range(2):
                    kaug = qkv[1, :, lanes] * half_mask(e) + kpat[e]
                    head_rows = pl.ds(pl.multiple_of(p * 128 + 64 * e, 64), 64)
                    for b in range(NT):
                        lo, hi = KEY_RANGE[b]
                        cols = slice(b * TILE, (b + 1) * TILE)
                        qaug = qkv[0, cols, lanes] * (half_mask(e) * 0.125) + qpat[e, cols, :]
                        st = mm_nt(kaug[lo:hi], qaug)
                        weights = jnp.exp(st - lse[pl.ds(2 * p + e, 1), cols])
                        pbuf[e, lo:hi, cols] = weights.astype(BF16)
                        goe = go[cols, lanes] * half_mask(e)
                        dp = mm_nt(vpair[lo:hi], goe)
                        ds = (weights * (dp - delta[pl.ds(2 * p + e, 1), cols])).astype(BF16)
                        dsbuf[e, lo:hi, cols] = ds
                        dqt[64 * e : 64 * e + 64, cols] = mm(kt[head_rows, lo:hi], ds)
                        if b == 0:
                            pbuf[e, hi:LEN, cols] = jnp.zeros((LEN - hi, TILE), BF16)
                            dsbuf[e, hi:LEN, cols] = jnp.zeros((LEN - hi, TILE), BF16)
                        if b == NT - 1:
                            pbuf[e, 0:lo, cols] = jnp.zeros((lo, TILE), BF16)
                            dsbuf[e, 0:lo, cols] = jnp.zeros((lo, TILE), BF16)
                keep = keep_row(128, cfg_ref[0, 1] * HDIM - p * 128)
                out_lanes = lanes_of(pp)
                for t in range(NT):
                    rows = slice(t * TILE, (t + 1) * TILE)
                    tg[rows, out_lanes] = (dqt[:, rows].T * (keep * 0.125)).astype(BF16)
                    dk = jnp.zeros((TILE, 128), F32)
                    dv = jnp.zeros((TILE, 128), F32)
                    for e in range(2):
                        dk = dk + mm(dsbuf[e, rows, :], qkv[0, :, lanes] * half_mask(e))
                        dv = dv + mm(pbuf[e, rows, :], go[:, lanes] * half_mask(e))
                    tg[rows, pl.ds(pl.multiple_of(256 + pp * 128, 128), 128)] = (
                        dk * (keep * 0.125)
                    ).astype(BF16)
                    tg[rows, pl.ds(pl.multiple_of(512 + pp * 128, 128), 128)] = (dv * keep).astype(
                        BF16
                    )

        i = new_slot()
        weight_grad(hlt, tg, gslot.at[i])
        send_slot(i, gu_out.at[j])
        span = slice(256 * j, 256 * j + 256)

        def back(t, bias, span=span):
            rows = rows_of(t)
            total = fg[rows, :]
            for i in range(3):
                total = total + mm_nt(tg[rows, 256 * i : 256 * i + 256], wa[i, :, span])
            fg[rows, :] = total
            return bias + col_sum(tg[rows, :].astype(F32))

        bias = lax.fori_loop(0, NT, back, zero)
        put(sg, "bq", bias[:, 0:256], 256 * j)
        put(sg, "bv", bias[:, 512:768], 256 * j)

    c_wp.wait()
    c_feat.wait()
    zero_feat = jnp.zeros((1, FEAT), F32)

    def first(t, sums):
        gain_sum, shift_sum, bias_sum = sums
        rows = rows_of(t)
        hat, inv, normed = norm0(feat, svec, rows)
        nrmt[:, rows] = normed.T
        low = (fg[rows, :] * keep_row(D, width)).astype(BF16)
        dg[rows, :] = low
        g = mm_nt(low, wp[...])
        gain_sum = gain_sum + col_sum(g * hat)
        shift_sum = shift_sum + col_sum(g)
        a = g * piece(svec, "g0")
        dx = inv * (a - row_sum(a) * (1.0 / FEAT) - hat * (row_sum(a * hat) * (1.0 / FEAT)))
        dxs[rows, :] = 0.1 * dx
        return gain_sum, shift_sum, bias_sum + col_sum(low.astype(F32))

    gain_sum, shift_sum, bias_sum = lax.fori_loop(0, NT, first, (zero_feat, zero_feat, zero))
    put(sg, "g0", gain_sum)
    put(sg, "b0", shift_sum)
    put(sg, "bp", bias_sum)
    c_dx = pltpu.make_async_copy(dxs, dx_out, sem_dx)
    c_dx.start()
    i = new_slot()
    weight_grad(nrmt, dg, gslot.at[i], FEAT // TILE)
    c_gp = pltpu.make_async_copy(gslot.at[i, 0:FEAT, :], gwp_out, sem_g.at[i])
    c_gp.start()
    c_dx.wait()
    slot_wait(1 - i)
    c_gp.wait()


def any_spec():
    return pl.BlockSpec(memory_space=pl.ANY)


def vmem_spec():
    return pl.BlockSpec(memory_space=pltpu.VMEM)


def smem_spec():
    return pl.BlockSpec(memory_space=pltpu.SMEM)


def forward_call(seg, cfg, feat, cot, wg, wp, svec, upto=9):
    shape = jax.ShapeDtypeStruct
    outs = [
        (shape((LEN, D), BF16), any_spec()),
        (shape((LEN, D), BF16), any_spec()),
        (shape((D, LEN), BF16), any_spec()),
        (shape((3, LEN, D), BF16), any_spec()),
        (shape((D, LEN), BF16), any_spec()),
        (shape((LEN, D), BF16), any_spec()),
        (shape((D, LEN), BF16), any_spec()),
        (shape((LEN, D), BF16), any_spec()),
        (shape((LEN, 128), F32), vmem_spec()),
        (shape((D, LEN), BF16), any_spec()),
        (shape((4, LEN, D), BF16), any_spec()),
        (shape((4, LEN, D), BF16), any_spec()),
        (shape((LEN, D), F32), any_spec()),
        (shape((LEN, D), BF16), any_spec()),
        (shape((D, LEN), BF16), any_spec()),
        (shape((16, LEN), F32), vmem_spec()),
        (shape((1, VEC), F32), vmem_spec()),
    ]
    bf = lambda *s: pltpu.VMEM(s, BF16)
    scratch = [
        bf(LEN, FEAT), bf(LEN, D), bf(12, D, D), bf(FEAT, D), pltpu.VMEM((LEN, D), F32),
        bf(LEN, D), bf(D, LEN), bf(3, LEN, D), bf(D, LEN), bf(D, LEN), bf(LEN, D), bf(D, LEN),
        bf(LEN, D), bf(LEN, D), bf(D, LEN), bf(4, LEN, D), bf(4, LEN, D), bf(LEN, D), bf(D, LEN),
        bf(LEN, D), bf(2, LEN, 128), bf(2, LEN, 128),
        pltpu.SemaphoreType.DMA((15,)), pltpu.SemaphoreType.DMA((24,)),
    ]
    return pl.pallas_call(
        functools.partial(forward_kernel, upto),
        out_shape=[o[0] for o in outs],
        in_specs=[smem_spec(), smem_spec()] + [any_spec()] * 4 + [vmem_spec()],
        out_specs=[o[1] for o in outs],
        scratch_shapes=scratch,
        compiler_params=pltpu.CompilerParams(vmem_limit_bytes=VMEM_LIMIT),
        name="forward",
    )(seg, cfg, feat, cot, wg, wp, svec)


def backward_call(seg, cfg, feat, wg, wp, svec, saved, upto=9):
    shape = jax.ShapeDtypeStruct
    bf = lambda *s: pltpu.VMEM(s, BF16)
    scratch = [
        bf(LEN, FEAT), bf(2, D, D), bf(2, D, D), bf(D, D), bf(3, D, D), bf(FEAT, D), bf(D, LEN),
        bf(3, LEN, D), bf(D, LEN), bf(LEN, D), bf(D, LEN), bf(LEN, D), pltpu.VMEM((LEN, 128), F32),
        bf(D, LEN), bf(2, LEN, D), bf(2, LEN, D), bf(LEN, D), pltpu.VMEM((LEN, D), F32),
        bf(LEN, D), bf(D, LEN), bf(LEN, D), bf(LEN, D), pltpu.VMEM((16, LEN), F32),
        pltpu.VMEM((128, LEN), F32), bf(2, LEN, LEN), bf(2, LEN, LEN), pltpu.VMEM((2, D, D), F32),
        pltpu.VMEM((LEN, FEAT), F32), bf(2, LEN, 128), bf(2, LEN, 128), bf(FEAT, LEN),
        pltpu.SemaphoreType.DMA((17,)), pltpu.SemaphoreType.DMA((2, 4)),
        pltpu.SemaphoreType.DMA((2,)), pltpu.SemaphoreType.DMA,
    ]
    return pl.pallas_call(
        functools.partial(backward_kernel, upto),
        out_shape=[
            shape((LEN, FEAT), F32), shape((12, D, D), F32), shape((FEAT, D), F32), shape((1, VEC), F32),
        ],
        in_specs=[smem_spec(), smem_spec()] + [any_spec()] * 3 + [vmem_spec()]
        + [any_spec()] * 13 + [vmem_spec()] * 2,
        out_specs=[any_spec()] * 3 + [vmem_spec()],
        scratch_shapes=scratch,
        compiler_params=pltpu.CompilerParams(vmem_limit_bytes=VMEM_LIMIT),
        name="backward",
    )(seg, cfg, feat, wg, wp, svec, *saved)


def adam(weight, moment, square, grad, rate):
    moment_new = BETA_ONE * moment + (1.0 - BETA_ONE) * grad
    square_new = BETA_TWO * square + (1.0 - BETA_TWO) * grad * grad
    fix_one = 1.0 - BETA_ONE**STEP
    fix_two = 1.0 - BETA_TWO**STEP
    direction = moment_new / fix_one / (jnp.sqrt(square_new / fix_two) + ADAM_EPS)
    return (moment_new, square_new, weight - rate * (direction + DECAY * weight))


AXES = ("grp", "dp")


def layer(features, lengths, config, cotangent, wg, wp, svec, upto=9, back_upto=9):
    feat = features.reshape(LEN, FEAT)
    cot = cotangent.reshape(LEN, D)
    saved = forward_call(lengths, config, feat, cot, wg, wp, svec, upto)
    activations = saved[0]
    dx, gu, gwp, sg = backward_call(lengths, config, feat, wg, wp, svec, saved[2:], back_upto)
    return activations, dx, gu, gwp, sg


def per_device(
    features, segment_lengths, subnet_config, cotangent,
    projection_weight, projection_moment, projection_square,
    attention_weight, attention_moment, attention_square,
    output_weight, output_moment, output_square,
    feedforward_weight, feedforward_moment, feedforward_square,
    small_params, small_moment, small_square,
):
    gather = lambda w, axis: lax.all_gather(w.astype(BF16), AXES, axis=axis, tiled=True)
    wp = gather(projection_weight, 0)
    wa = gather(attention_weight, 1)
    wo = gather(output_weight, 0)
    wf = gather(feedforward_weight, 1)
    svec = gather(small_params, 0).astype(F32).reshape(1, VEC)
    quarters = wf.reshape(2, D, 4, D).transpose(0, 2, 1, 3).reshape(8, D, D)
    wg = jnp.concatenate([wa, wo[None], quarters], 0)
    activations, dx, gu, gwp, sg = layer(
        features, segment_lengths, subnet_config, cotangent, wg, wp, svec
    )
    ga = gu[0:3].reshape(3, D, 3, 256).transpose(2, 1, 0, 3).reshape(3, D, D)
    gf = gu[4:12].reshape(2, 4, D, D).transpose(0, 2, 1, 3).reshape(2, D, FF)
    scatter = lambda g, dim: lax.psum_scatter(g, AXES, scatter_dimension=dim, tiled=True)
    gp = scatter(gwp, 0)
    ga = scatter(ga, 1)
    go = scatter(gu[3], 0)
    gf = scatter(gf, 1)
    gs = scatter(sg.reshape(VEC), 0)
    out = [activations.reshape(1, LEN, D), dx.reshape(1, LEN, FEAT)]
    for w, m, v, g, rate in (
        (projection_weight, projection_moment, projection_square, gp, RATE),
        (attention_weight, attention_moment, attention_square, ga, RATE),
        (output_weight, output_moment, output_square, go, RATE),
        (feedforward_weight, feedforward_moment, feedforward_square, gf, RATE),
        (small_params, small_moment, small_square, gs, SMALL_RATE),
    ):
        out.append(g)
        out.extend(adam(w, m, v, g, rate))
    return tuple(out)


def solution(mesh):
    rows3, rows2, stacked, flat = (
        P(AXES, None, None), P(AXES, None), P(None, AXES, None), P(AXES),
    )
    return jax.shard_map(
        per_device,
        mesh=mesh,
        in_specs=(
            rows3, rows2, P("grp", None), rows3, rows2, rows2, rows2, stacked, stacked, stacked,
            rows2, rows2, rows2, stacked, stacked, stacked, flat, flat, flat,
        ),
        out_specs=(rows3, rows3) + (rows2,) * 4 + (stacked,) * 4 + (rows2,) * 4 + (stacked,) * 4 + (flat,) * 4,
        check_vma=False,
    )
```

time: 1200 us -> 1030 us (0.86)
  matrix products: 429 us -> 0 us
  Pallas kernels: 0 us -> 171 us
  waiting for transfers between devices: 503 us -> 618 us
  other arithmetic: 73.1 us -> 30.7 us
    dot_general x27 -> x0, matrix products: 429 us -> none  [the longest x2 105 us: attend_back(): jnp.einsum('hqk,qhd->khd', raw_grad, block_query, preferred_element_type=...]
    pallas_call x0 -> x2, Pallas kernels: none -> 171 us  [the longest x1 97.2 us: backward_call(): pl.pallas_call(functools.partial(backward_kernel, upto), out_shape=[shape...]
    all_gather x3, waiting for transfers between devices: 18 us -> 104 us  [per_device(): lax.all_gather(w.astype(BF16), AXES, axis=axis, tiled=True)]
    reduce_sum x13 -> x0, other arithmetic: 37.6 us -> none  [the longest x1 21.6 us: attend_row(): summed = jnp.sum(powers, -1, keepdims=True)]
    reduce_scatter x3, waiting for transfers between devices: 290 us -> 318 us  [per_device(): lax.psum_scatter(g, AXES, scatter_dimension=dim, tiled=True)]
    unnamed x184 -> x35, local copies, waits for them, and re-layouts: 28.1 us -> 1.92 us
    slice x8 -> x4, local copies, waits for them, and re-layouts: 3.98 us -> 26 us  [the longest x2 14.6 us: per_device(): ga = gu[0:3].reshape(3, D, 3, 256).transpose(2, 1, 0, 3).reshape(3, D, D)]
    reshape x0 -> x3, local copies, waits for them, and re-layouts: none -> 18.3 us  [the longest x1 10.5 us: per_device(): ga = gu[0:3].reshape(3, D, 3, 256).transpose(2, 1, 0, 3).reshape(3, D, D)]
  transfers between devices with their start and end apart: 7 -> 7, of which waited for: 4 -> 6; matrix products, arithmetic and copies ran while one was open for 15% -> 7% of each run, Pallas kernels for 0% -> 0%
where the time goes in v1:
time: 1030 us; the launch traced here: 1020 us
  waiting for transfers between devices  618 us (60%)
  Pallas kernels  171 us (17%)
  blocking collectives  132 us (13%)
  local copies, waits for them, and re-layouts  55.8 us (5%)
  other arithmetic  30.7 us (3%)
  between operations  14.6 us (1%)
    reduce_scatter x3, waiting for transfers between devices, per_device(): lax.psum_scatter(g, AXES, scatter_dimension=dim, tiled=True)  318 us
    unnamed x8, waiting for transfers between devices  195 us
    all_gather x3, waiting for transfers between devices, per_device(): lax.all_gather(w.astype(BF16), AXES, axis=axis, tiled=True)  104 us
    pallas_call x1, Pallas kernels, backward_call(): pl.pallas_call(functools.partial(backward_kernel, upto), out_shape=[shape...  97.2 us
    unnamed x2, blocking collectives  82.1 us
    pallas_call x1, Pallas kernels, forward_call(): pl.pallas_call(functools.partial(forward_kernel, upto), out_shape=[o[0] f...  73.7 us
    all_gather x1, blocking collectives, per_device(): lax.all_gather(w.astype(BF16), AXES, axis=axis, tiled=True)  50.4 us
  transfers between devices with their start and end apart: 7, of which 6 were waited for; matrix products, arithmetic and copies ran while one was open for 7% of the time, Pallas kernels for 0%

profile of v1, /device:TPU:0, one launch (start us, length us, event | category | flops | bytes accessed | tf_op | source)
XLA Modules:
  0.0 1022.5 jit_solution(1842925269483662519)
XLA Ops:
  7.2 1.8 convert_element_type.18
  10.7 1.6 convert_element_type.16
  14.1 42.9 %all-reduce = bf16[11008]{0:T(1024)(128)(2,1)S(1)} all-reduce(bf16[11008]{0:T(1024)(128)(2,1)S(1)} %dynamic-update-slice), channel_id=1, replica_groups=mesh['grp'=4,'dp'=8] {'grp','dp'}, use_global_device_ids=true, to_apply=%add | all-reduce | flops 11008 | bytes 44032
  57.6 50.4 %all_gather.18.wp_hbm = bf16[512,768]{1,0:T(8,128)(2,1)} all-gather(bf16[16,768]{1,0:T(8,128)(2,1)S(1)} %convert_element_type.19), channel_id=1, replica_groups=mesh['grp'=4,'dp'=8] {'grp','dp'}, dimensions={0}, use_global_device_ids=true | all-gather | bytes 811008 | tf_op jit(solution)/shard_map/all_gather | solution.py:669
  108.0 4.1 fusion.10
  112.1 4.2 pad_maximum_fusion.1
  116.3 41.4 %all-gather.6.cloned.1.call-done = bf16[768,768]{1,0:T(8,128)(2,1)} async-done(((bf16[24,768]{1,0:T(8,128)(2,1)}), bf16[768,768]{1,0:T(8,128)(2,1)}) %all-gather.6.cloned.1.call-update) | async-done | bytes 1179664 | tf_op jit(solution)/shard_map/all_gather | solution.py:669
  157.7 63.1 %all-gather.4.cloned.1.call-done = bf16[3,768,768]{2,1,0:T(8,128)(2,1)} async-done(((bf16[3,24,768]{2,1,0:T(8,128)(2,1)}), bf16[3,768,768]{2,1,0:T(8,128)(2,1)}) %all-gather.4.cloned.1.call-update) | async-done | bytes 3538960 | tf_op jit(solution)/shard_map/all_gather | solution.py:669
  220.8 12.7 %pad_maximum_fusion.wg_hbm = bf16[12,768,768]{2,1,0:T(8,128)(2,1)} fusion(bf16[8,768,768]{2,1,0:T(8,128)(2,1)} %bitcast.19, bf16[1,768,768]{2,1,0:T(8,128)(2,1)} %bitcast.25, bf16[3,768,768]{2,1,0:T(8,128)(2,1)} %all-gather.4.cloned.1.call-done), kind=kLoop, calls=%fused_computation | loop fusion | flops 14155776 | bytes 28311552 | tf_op jit(solution)/shard_map/concatenate | solution.py:676
  233.4 73.7 %forward.1 = (bf16[1024,768]{1,0:T(8,128)(2,1)}, bf16[1024,768]{1,0:T(8,128)(2,1)}, bf16[768,1024]{1,0:T(8,128)(2,1)}, bf16[3,1024,768]{2,1,0:T(8,128)(2,1)}, bf...) custom-call(s32[1,4]{1,0:T(1,128)} %seg_ref.3, ...), custom_call_target="tpu_custom_call" | custom-call | tf_op jit(solution)/shard_map/forward/pallas_call | solution.py:602
  307.2 97.2 %backward.1 = (f32[1024,512]{1,0:T(8,128)}, f32[12,768,768]{2,1,0:T(8,128)}, f32[512,768]{1,0:T(8,128)}, f32[1,11008]{1,0:T(1,128)}) custom-call(s32[1,4]{1,0:T(1,128)} %seg_ref.3, s32[1,3]{1,0:T(1,128)} %cfg_ref.3, bf16[1024,512]{1,0:T(8,128)(2,1)} %bitcast.23, bf16[12,768,768]{2,1,0:T(8,128)(2,1)} %pad_maximum_fusion.wg_hbm, ...), custom_call_target="tpu_custom_call" | custom-call | tf_op jit(solution)/shard_map/backward/pallas_call | solution.py:626
  404.5 3.2 slice_bitcast_fusion
  407.8 6.4 slice.25
  414.2 8.2 copy.66
  422.3 6.4 copy.67
  428.7 10.5 %copy.68 = f32[3,768,768]{2,0,1:T(4,128)} copy(f32[3,768,768]{1,2,0:T(8,128)} %bitcast.21) | data formatting | bytes 14155776 | tf_op jit(solution)/shard_map/reshape | solution.py:680
  439.2 7.3 slice.27
  446.6 7.2 copy.74
  454.7 39.2 %all-reduce.2 = f32[11008]{0:T(1024)S(1)} all-reduce(f32[11008]{0:T(1024)S(1)} %reduce), channel_id=6, replica_groups=mesh['grp'=4,'dp'=8] {'grp','dp'}, use_global_device_ids=true, to_apply=%region_4.0.clone | all-reduce | flops 11008 | bytes 88064
  494.6 5.8 reduce-scatter.4.cloned.1.call-done
  501.9 102.4 %reduce-scatter.6.cloned.1.call-done = f32[24,768]{1,0:T(8,128)} async-done(((f32[768,768]{1,0:T(8,128)}), f32[24,768]{1,0:T(8,128)}) %reduce-scatter.6.cloned.1.call-update) | async-done | bytes 73744 | tf_op jit(solution)/shard_map/reduce_scatter | solution.py:682
  605.9 194.9 %all-reduce.5.cloned.1.call-done = f32[3,768,768]{2,0,1:T(4,128)} async-done(((f32[3,768,768]{2,0,1:T(4,128)}), f32[3,768,768]{2,0,1:T(4,128)}) %all-reduce.5.cloned.1.call-update) | async-done | bytes 7077904
  802.8 210.1 %reduce-scatter.8.cloned.1.call-done = f32[2,24,3072]{2,1,0:T(8,128)} async-done(((f32[2,768,3072]{2,1,0:T(8,128)}), f32[2,24,3072]{2,1,0:T(8,128)}) %reduce-scatter.8.cloned.1.call-update) | async-done | bytes 589840 | tf_op jit(solution)/shard_map/reduce_scatter | solution.py:682
  1012.9 2.6 multiply_subtract_fusion
  (59 shorter events, 10.8 us)
Async XLA Ops:
  7.2 100.8 %all-gather.8.cloned.1.call-start = ((), (), s32[]{:S(2)}) async-start(), calls=%async_computation.5 | async-start | bytes 9732096 | tf_op jit(solution)/shard_map/all_gather | solution.py:669
  9.1 148.6 %all-gather.6.cloned.1.call-start = ((), (), s32[]{:S(2)}) async-start(), calls=%async_computation.4 | async-start | bytes 1216512 | tf_op jit(solution)/shard_map/all_gather | solution.py:669
  10.7 210.1 %all-gather.4.cloned.1.call-start = ((), (), s32[]{:S(2)}) async-start(), calls=%async_computation.3 | async-start | bytes 3649536 | tf_op jit(solution)/shard_map/all_gather | solution.py:669
  12.3 488.1 %reduce-scatter.4.cloned.1.call-start = ((), (), s32[]{:S(2)}) async-start(), calls=%async_computation.6 | async-start | bytes 1622016 | tf_op jit(solution)/shard_map/reduce_scatter | solution.py:682
  404.4 199.9 %reduce-scatter.6.cloned.1.call-start = ((), (), s32[]{:S(2)}) async-start(), calls=%async_computation.7 | async-start | bytes 2433024 | tf_op jit(solution)/shard_map/reduce_scatter | solution.py:682
  407.7 393.1 %all-reduce.5.cloned.1.call-start = ((), (), s32[]{:S(2)}) async-start(), calls=%async_computation.9 | async-start | bytes 18874368
  439.2 573.7 %reduce-scatter.8.cloned.1.call-start = ((), (), s32[]{:S(2)}) async-start(), calls=%async_computation.8 | async-start | bytes 19464192 | tf_op jit(solution)/shard_map/reduce_scatter | solution.py:682
  453.8 0.8 copy-start.12
  453.8 40.1 %copy-start.13 = (f32[344]{0:T(512)S(1)}, f32[344]{0:T(512)}, u32[]{:S(2)}) copy-start(f32[344]{0:T(512)} %param.35) | copy-start | bytes 4132
  453.8 40.1 %copy-start.14 = (f32[344]{0:T(512)S(1)}, f32[344]{0:T(512)}, u32[]{:S(2)}) copy-start(f32[344]{0:T(512)} %param.37) | copy-start | bytes 4132
  453.8 40.1 %copy-start.15 = (f32[344]{0:T(512)S(1)}, f32[344]{0:T(512)}, u32[]{:S(2)}) copy-start(f32[344]{0:T(512)} %param.36) | copy-start | bytes 4132
  453.8 46.7 %copy-start.7 = (f32[16,768]{1,0:T(8,128)S(1)}, f32[16,768]{1,0:T(8,128)}, u32[]{:S(2)}) copy-start(f32[16,768]{1,0:T(8,128)} %param.23) | copy-start | bytes 147460
  453.8 46.6 %copy-start.10 = (f32[16,768]{1,0:T(8,128)S(1)}, f32[16,768]{1,0:T(8,128)}, u32[]{:S(2)}) copy-start(f32[16,768]{1,0:T(8,128)} %param.25) | copy-start | bytes 147460
  453.8 46.6 %copy-start.11 = (f32[16,768]{1,0:T(8,128)S(1)}, f32[16,768]{1,0:T(8,128)}, u32[]{:S(2)}) copy-start(f32[16,768]{1,0:T(8,128)} %param.24) | copy-start | bytes 147460
  453.8 150.5 %copy-start.4 = (f32[24,768]{1,0:T(8,128)S(1)}, f32[24,768]{1,0:T(8,128)}, u32[]{:S(2)}) copy-start(f32[24,768]{1,0:T(8,128)} %param.29) | copy-start | bytes 221188
  453.8 150.5 %copy-start.8 = (f32[24,768]{1,0:T(8,128)S(1)}, f32[24,768]{1,0:T(8,128)}, u32[]{:S(2)}) copy-start(f32[24,768]{1,0:T(8,128)} %param.31) | copy-start | bytes 221188
  453.8 150.5 %copy-start.9 = (f32[24,768]{1,0:T(8,128)S(1)}, f32[24,768]{1,0:T(8,128)}, u32[]{:S(2)}) copy-start(f32[24,768]{1,0:T(8,128)} %param.30) | copy-start | bytes 221188
  453.9 348.0 %copy-start.1 = (f32[3,24,768]{2,1,0:T(8,128)S(1)}, f32[3,24,768]{2,1,0:T(8,128)}, u32[]{:S(2)}) copy-start(f32[3,24,768]{2,1,0:T(8,128)} %param.26) | copy-start | bytes 663556
  453.9 348.0 %copy-start.5 = (f32[3,24,768]{2,1,0:T(8,128)S(1)}, f32[3,24,768]{2,1,0:T(8,128)}, u32[]{:S(2)}) copy-start(f32[3,24,768]{2,1,0:T(8,128)} %param.28) | copy-start | bytes 663556
  453.9 348.0 %copy-start.6 = (f32[3,24,768]{2,1,0:T(8,128)S(1)}, f32[3,24,768]{2,1,0:T(8,128)}, u32[]{:S(2)}) copy-start(f32[3,24,768]{2,1,0:T(8,128)} %param.27) | copy-start | bytes 663556
  453.9 559.0 %copy-start = (f32[2,24,3072]{2,1,0:T(8,128)S(1)}, f32[2,24,3072]{2,1,0:T(8,128)}, u32[]{:S(2)}) copy-start(f32[2,24,3072]{2,1,0:T(8,128)} %param.32) | copy-start | bytes 1769476
  453.9 559.0 %copy-start.2 = (f32[2,24,3072]{2,1,0:T(8,128)S(1)}, f32[2,24,3072]{2,1,0:T(8,128)}, u32[]{:S(2)}) copy-start(f32[2,24,3072]{2,1,0:T(8,128)} %param.34) | copy-start | bytes 1769476
  453.9 559.0 %copy-start.3 = (f32[2,24,3072]{2,1,0:T(8,128)S(1)}, f32[2,24,3072]{2,1,0:T(8,128)}, u32[]{:S(2)}) copy-start(f32[2,24,3072]{2,1,0:T(8,128)} %param.33) | copy-start | bytes 1769476
Sparse Core Ops, SparseCore 0:
  11.8 88.7 all-gather.7
  104.2 53.4 all-gather.5
  161.4 59.2 all-gather.3
  404.6 95.8 reduce-scatter.3
  506.1 98.1 reduce-scatter.5
  610.9 189.8 all-reduce.4
  807.8 205.0 reduce-scatter.7
